TPU v7x, 32 devices: a whole 2x2x4 slice. The times are simulated.
32 devices in a mesh: gz: 2 (over y), gy: 4 (over x, core), gx: 4 (over z).
Axes of the slice: x: 2, y: 2, z: 4, core: 2. Of those that a mesh axis runs over, the one named last changes fastest.
Arguments:
- labels: int32 [2, 32, 512], P('gz', 'gy', 'gx'), may hold values from 0 to 7
- tissue_tensors: float32 [6, 8], replicated, as said below
- electrodes: int32 [2, 64], replicated, may hold values from 0 to 32767, as said below
- initial: float32 [64, 2, 32, 512], P(None, 'gz', 'gy', 'gx'), may hold values from -4 to 4
Outputs:
- solution: float32 [64, 2, 32, 512], P(None, 'gz', 'gy', 'gx')
- residual: float32 [64, 2, 32, 512], P(None, 'gz', 'gy', 'gx')
Inputs may be any that keep to these rules, and one draw needn't show every extreme that they name: `tissue_tensors`: the tensors are symmetric and positive definite: each off-diagonal component is at most 0.3 times the geometric mean of its two diagonal components. `electrodes`: all 128 voxel indices are distinct; voxel (z, y, x) has index (z * 32 + y) * 512 + x.
All inputs are finite; a program needn't handle non-finite values.
Results may differ from a plain program's by a relative error of at most 0.0003.
Values sent between devices are 32-bit elements; how exact they have to be, the bound alone decides.
A program may use at most 64 MiB of HBM per device.

v0:
```python
import jax
import jax.numpy as jnp
from jax import lax
from jax.sharding import PartitionSpec as P

ITERS = 2


def from_behind(value, axis, steps):
    count = lax.axis_size(axis)
    initial, last = (max(0, -steps), min(count, count - steps))
    return lax.ppermute(value, axis, [(source, source + steps) for source in range(initial, last)])


def padded_2(block, sides, width):
    for axis, dim in sides:
        count = lax.axis_size(axis)
        forward = [(i, i + 1) for i in range(count - 1)]
        backward = [(target, source) for source, target in forward]
        low = lax.ppermute(
            lax.slice_in_dim(block, block.shape[dim] - width, None, axis=dim), axis, forward
        )
        high = lax.ppermute(lax.slice_in_dim(block, 0, width, axis=dim), axis, backward)
        block = jnp.concatenate([low, block, high], axis=dim)
    return block


def tensor_lookup(labels, table):
    result = jnp.zeros((6,) + labels.shape, jnp.float32)
    for tissue in range(table.shape[1]):
        result = result + jnp.where(
            labels[None] == tissue, table[:, tissue][:, None, None, None], jnp.float32(0.0)
        )
    return result


def flux_terms(tensor, grad_x, grad_y, grad_z):
    flux_x = tensor[0] * grad_x + tensor[3] * grad_y + tensor[4] * grad_z
    flux_y = tensor[3] * grad_x + tensor[1] * grad_y + tensor[5] * grad_z
    flux_z = tensor[4] * grad_x + tensor[5] * grad_y + tensor[2] * grad_z
    return (flux_x, flux_y, flux_z)


def lower_box(tensor):
    below_z = from_behind(tensor, "gz", 1)
    below_y = from_behind(tensor[:, :, -1:], "gy", 1)
    below_x = from_behind(tensor[:, :, :, -1:], "gx", 1)
    inner = jnp.concatenate([below_x, tensor], axis=3)
    side_y = jnp.pad(below_y, ((0, 0), (0, 0), (0, 0), (1, 0)))
    inner = jnp.concatenate([side_y, inner], axis=2)
    side_z = jnp.pad(below_z, ((0, 0), (0, 0), (1, 0), (1, 0)))
    return jnp.concatenate([side_z, inner], axis=1)


def operate_faces(direction, tensor_box):
    padded = padded_2(direction, (("gz", 1), ("gy", 2), ("gx", 3)), 1)
    centre = padded[:, :-1, :-1, :-1]
    grad_z = padded[:, 1:, :-1, :-1] - centre
    grad_y = padded[:, :-1, 1:, :-1] - centre
    grad_x = padded[:, :-1, :-1, 1:] - centre
    flux_x, flux_y, flux_z = flux_terms(tensor_box, grad_x, grad_y, grad_z)
    return (
        flux_z[:, :-1, 1:, 1:]
        - flux_z[:, 1:, 1:, 1:]
        + (flux_y[:, 1:, :-1, 1:] - flux_y[:, 1:, 1:, 1:])
        + (flux_x[:, 1:, 1:, :-1] - flux_x[:, 1:, 1:, 1:])
    )


def gram_of(first, second):
    leads = first.shape[0]
    return lax.dot_general(
        first.reshape(leads, -1),
        second.reshape(leads, -1),
        (((1,), (1,)), ((), ())),
        precision=lax.Precision.HIGHEST,
        preferred_element_type=jnp.float32,
    )


def combine_rows(coef, field):
    leads = field.shape[0]
    return jnp.dot(
        coef.T,
        field.reshape(leads, -1),
        precision=lax.Precision.HIGHEST,
        preferred_element_type=jnp.float32,
    ).reshape(field.shape)


def factor_solve(matrix, target):
    factor = jnp.linalg.cholesky(matrix)
    halfway = lax.linalg.triangular_solve(factor, target, left_side=True, lower=True)
    return lax.linalg.triangular_solve(
        factor, halfway, left_side=True, lower=True, transpose_a=True
    )


def body(labels, tissue_tensors, electrodes, initial):
    cells_z, cells_y, cells_x = labels.shape
    rows_all = cells_y * lax.axis_size("gy")
    cols_all = cells_x * lax.axis_size("gx")
    depth_ids = lax.axis_index("gz") * cells_z + lax.broadcasted_iota(jnp.int32, labels.shape, 0)
    row_ids = lax.axis_index("gy") * cells_y + lax.broadcasted_iota(jnp.int32, labels.shape, 1)
    col_ids = lax.axis_index("gx") * cells_x + lax.broadcasted_iota(jnp.int32, labels.shape, 2)
    voxel_id = (depth_ids * rows_all + row_ids) * cols_all + col_ids
    sources = (voxel_id[None] == electrodes[0][:, None, None, None]).astype(jnp.float32) - (
        voxel_id[None] == electrodes[1][:, None, None, None]
    ).astype(jnp.float32)
    tensor = tensor_lookup(labels, tissue_tensors)
    tensor_box = lower_box(tensor)

    def operate(field):
        return operate_faces(field, tensor_box)

    solution = initial
    residual = sources - operate(initial)
    direction = residual
    rr_now = lax.psum(gram_of(residual, residual), ("gz", "gy", "gx"))
    for iteration in range(ITERS):
        image = operate(direction)
        curve = lax.psum(gram_of(direction, image), ("gz", "gy", "gx"))
        step_coef = factor_solve(curve, rr_now)
        solution = solution + combine_rows(step_coef, direction)
        residual = residual - combine_rows(step_coef, image)
        if iteration + 1 < ITERS:
            rr_next = lax.psum(gram_of(residual, residual), ("gz", "gy", "gx"))
            beta_coef = factor_solve(rr_now, rr_next)
            direction = residual + combine_rows(beta_coef, direction)
            rr_now = rr_next
    return (solution, residual)


def solution(mesh):
    placed = (P("gz", "gy", "gx"), P(), P(), P(None, "gz", "gy", "gx"))
    return jax.shard_map(
        body,
        mesh=mesh,
        in_specs=placed,
        out_specs=(P(None, "gz", "gy", "gx"), P(None, "gz", "gy", "gx")),
        check_vma=False,
    )
```

profile of v0, /device:TPU:0, one launch (start us, length us, event | category | flops | bytes accessed | tf_op | source)
XLA Modules:
  0.0 279.7 jit_solution(1200948065979888118)
XLA Ops:
  1.7 4.9 %collective-permute-start.3 = (f32[64,1,8,128]{3,0,2,1:T(8,128)S(1)}, f32[64,1,8,128]{3,0,2,1:T(8,128)S(1)}, u32[]{:S(2)}, u32[]{:S(2)}) collective-permute-start(f32[64,1,8,128]{3,0,2,1:T(8,128)S(1)} %copy.64), channel_id=1, source_target_pairs={{0,16},{1,17},{2,18},{3,19},{4,20},{5,21},{6,22},{7,23},{8,24},{9,... | collective-permute-start | bytes 786440 | tf_op jit(solution)/shard_map/ppermute | solution.py:20
  6.6 1.3 collective-permute-start.4
  10.0 4.6 %collective-permute-start = (f32[6,1,8,128]{3,2,1,0:T(8,128)S(1)}, f32[6,1,8,128]{3,2,1,0:T(8,128)S(1)}, u32[]{:S(2)}, u32[]{:S(2)}) collective-permute-start(f32[6,1,8,128]{3,2,1,0:T(8,128)S(1)} %select_add_fusion), channel_id=1, source_target_pairs={{0,16},{1,17},{2,18},{3,19},{4,20},{5,21},{6,22},{7,23},{8,24},{9,... | collective-permute-start | bytes 73736 | tf_op jit(solution)/shard_map/ppermute | solution.py:12
  14.6 3.5 %collective-permute-start.2 = (f32[6,1,8,1]{3,2,1,0:T(8,128)S(1)}, f32[6,1,8,1]{3,2,1,0:T(8,128)S(1)}, u32[]{:S(2)}, u32[]{:S(2)}) collective-permute-start(f32[6,1,8,1]{3,2,1,0:T(8,128)S(1)} %slice.282), channel_id=1, source_target_pairs={{0,1},{1,2},{2,3},{4,5},{5,6},{6,7},{8,9},{9,10},{10,11},{12,13},{... | collective-permute-start | bytes 584 | tf_op jit(solution)/shard_map/ppermute | solution.py:12
  20.4 4.1 %collective-permute-start.5 = (f32[64,3,1,128]{3,0,2,1:T(8,128)S(1)}, f32[64,3,1,128]{3,0,2,1:T(8,128)S(1)}, u32[]{:S(2)}, u32[]{:S(2)}) collective-permute-start(f32[64,3,1,128]{3,0,2,1:T(8,128)S(1)} %get-tuple-element.43), channel_id=1, source_target_pairs={{0,4},{4,8},{8,12},{1,5},{5,9},{9,13},{2,6},{6,10},{10,14},{3,7},{... | collective-permute-start | bytes 294920 | tf_op jit(solution)/shard_map/ppermute | solution.py:20
  24.6 1.3 collective-permute-start.6
  26.1 1.7 collective-permute-done.6
  29.2 3.5 %collective-permute-start.8 = (f32[64,3,10,1]{0,3,2,1:T(1,128)}, f32[64,3,10,1]{0,3,2,1:T(1,128)S(1)}, u32[]{:S(2)}, u32[]{:S(2)}) collective-permute-start(f32[64,3,10,1]{0,3,2,1:T(1,128)} %copy.52), channel_id=1, source_target_pairs={{0,1},{1,2},{2,3},{4,5},{5,6},{6,7},{8,9},{9,10},{10,11},{12,13},{... | collective-permute-start | bytes 23048 | tf_op jit(solution)/shard_map/ppermute | solution.py:20
  33.6 1.3 collective-permute-start.7
  34.9 1.3 copy.53
  36.3 1.8 maximum_maximum_fusion
  39.3 1.3 copy.51
  40.6 1.5 multiply_add_fusion.8
  43.2 1.3 collective-permute-start.10
  44.5 4.6 %collective-permute-start.9 = (f32[64,1,8,128]{3,0,2,1:T(8,128)S(1)}, f32[64,1,8,128]{3,0,2,1:T(8,128)S(1)}, u32[]{:S(2)}, u32[]{:S(2)}) collective-permute-start(f32[64,1,8,128]{3,0,2,1:T(8,128)S(1)} %fusion.21), channel_id=1, source_target_pairs={{0,16},{1,17},{2,18},{3,19},{4,20},{5,21},{6,22},{7,23},{8,24},{9,... | collective-permute-start | bytes 786440 | tf_op jit(solution)/shard_map/ppermute | solution.py:20
  49.1 4.9 %collective-permute-done.10 = f32[64,1,8,128]{3,0,2,1:T(8,128)S(1)} collective-permute-done((f32[64,1,8,128]{3,0,2,1:T(8,128)S(1)}, f32[64,1,8,128]{3,0,2,1:T(8,128)S(1)}, u32[]{:S(2)}, u32[]{:S(2)}) %collective-permute-start.10) | collective-permute-done | bytes 262176 | tf_op jit(solution)/shard_map/ppermute | solution.py:23
  54.0 1.7 collective-permute-done.9
  55.7 2.2 collective-permute-start.11
  57.9 1.3 collective-permute-start.12
  59.2 1.9 collective-permute-done.12
  61.8 3.4 %collective-permute-start.14 = (f32[64,3,10,1]{0,3,2,1:T(1,128)S(1)}, f32[64,3,10,1]{0,3,2,1:T(1,128)S(1)}, u32[]{:S(2)}, u32[]{:S(2)}) collective-permute-start(f32[64,3,10,1]{0,3,2,1:T(1,128)S(1)} %copy.56), channel_id=1, source_target_pairs={{0,1},{1,2},{2,3},{4,5},{5,6},{6,7},{8,9},{9,10},{10,11},{12,13},{... | collective-permute-start | bytes 23048 | tf_op jit(solution)/shard_map/ppermute | solution.py:20
  68.6 1.3 copy.57
  70.0 1.8 maximum_maximum_fusion.1
  71.8 1.5 collective-permute-done.13
  73.3 2.0 copy.55
  75.3 1.5 multiply_add_fusion.5
  78.5 42.6 %all-reduce.2 = (f32[64,64]{0,1:T(8,128)S(1)}, f32[64,64]{0,1:T(8,128)S(1)}) all-reduce(f32[64,64]{0,1:T(8,128)S(1)} %copy-done.22, f32[64,64]{0,1:T(8,128)S(1)} %convolution_bitcast_fusion.11), channel_id=1, replica_groups=mesh['gz'=2,'gy'=4,'gx'=4] {'gz','gy','gx'}, use_global_device_ids=true, to_apply=%region_3.5 | all-reduce | flops 8192 | bytes 65536 | tf_op jit(solution)/shard_map/psum | solution.py:119
  121.3 5.8 %cholesky.70 = f32[64,64]{1,0:T(8,128)S(1)} custom-call(f32[64,64]{1,0:T(8,128)S(1)} %get-tuple-element.61), custom_call_target="Cholesky" | custom-call | tf_op jit(solution)/shard_map/jit(cholesky)/cholesky | solution.py:92
  128.5 4.9 %custom-call.15 = f32[1,64,64]{1,2,0:T(8,128)S(1)} custom-call(f32[1,64,64]{2,1,0:T(8,128)S(1)} %fusion.34), custom_call_target="InvertDiagBlocksLowerTriangular" | custom-call | tf_op jit(solution)/shard_map/triangular_solve/custom-call.2 | solution.py:94
  133.4 5.9 %cholesky.59 = f32[64,64]{1,0:T(8,128)S(1)} custom-call(f32[64,64]{1,0:T(8,128)S(1)} %get-tuple-element.62), custom_call_target="Cholesky" | custom-call | tf_op jit(solution)/shard_map/jit(cholesky)/cholesky | solution.py:92
  140.6 4.9 %custom-call.13 = f32[1,64,64]{1,2,0:T(8,128)S(1)} custom-call(f32[1,64,64]{2,1,0:T(8,128)S(1)} %fusion.33), custom_call_target="InvertDiagBlocksLowerTriangular" | custom-call | tf_op jit(solution)/shard_map/triangular_solve/custom-call.2 | solution.py:94
  146.8 38.9 %psum.30 = f32[64,64]{1,0:T(8,128)S(1)} all-reduce(f32[64,64]{1,0:T(8,128)S(1)} %convolution_bitcast_fusion.9), channel_id=1, replica_groups=mesh['gz'=2,'gy'=4,'gx'=4] {'gz','gy','gx'}, use_global_device_ids=true, to_apply=%region_4.8 | all-reduce | flops 4096 | bytes 32768 | tf_op jit(solution)/shard_map/psum | solution.py:127
  186.6 4.2 %collective-permute-start.15 = (f32[64,1,8,128]{3,0,2,1:T(8,128)S(1)}, f32[64,1,8,128]{3,0,2,1:T(8,128)S(1)}, u32[]{:S(2)}, u32[]{:S(2)}) collective-permute-start(f32[64,1,8,128]{3,0,2,1:T(8,128)S(1)} %fusion.6), channel_id=1, source_target_pairs={{0,16},{1,17},{2,18},{3,19},{4,20},{5,21},{6,22},{7,23},{8,24},{9,... | collective-permute-start | bytes 786440 | tf_op jit(solution)/shard_map/ppermute | solution.py:20
  190.9 1.3 collective-permute-start.16
  192.2 3.9 %collective-permute-done.15 = f32[64,1,8,128]{3,0,2,1:T(8,128)S(1)} collective-permute-done((f32[64,1,8,128]{3,0,2,1:T(8,128)S(1)}, f32[64,1,8,128]{3,0,2,1:T(8,128)S(1)}, u32[]{:S(2)}, u32[]{:S(2)}) %collective-permute-start.15) | collective-permute-done | bytes 262176 | tf_op jit(solution)/shard_map/ppermute | solution.py:20
  196.0 4.1 %collective-permute-done.16 = f32[64,1,8,128]{3,0,2,1:T(8,128)S(1)} collective-permute-done((f32[64,1,8,128]{3,0,2,1:T(8,128)S(1)}, f32[64,1,8,128]{3,0,2,1:T(8,128)S(1)}, u32[]{:S(2)}, u32[]{:S(2)}) %collective-permute-start.16) | collective-permute-done | bytes 262176 | tf_op jit(solution)/shard_map/ppermute | solution.py:23
  200.2 1.3 collective-permute-start.17
  201.5 1.3 collective-permute-start.18
  202.8 2.9 %collective-permute-done.18 = f32[64,3,1,128]{3,0,2,1:T(8,128)S(1)} collective-permute-done((f32[64,3,1,128]{3,0,2,1:T(8,128)S(1)}, f32[64,3,1,128]{3,0,2,1:T(8,128)S(1)}, u32[]{:S(2)}, u32[]{:S(2)}) %collective-permute-start.18) | collective-permute-done | bytes 98336 | tf_op jit(solution)/shard_map/ppermute | solution.py:23
  207.2 3.3 %collective-permute-start.20 = (f32[64,3,10,1]{0,3,2,1:T(1,128)S(1)}, f32[64,3,10,1]{0,3,2,1:T(1,128)S(1)}, u32[]{:S(2)}, u32[]{:S(2)}) collective-permute-start(f32[64,3,10,1]{0,3,2,1:T(1,128)S(1)} %copy.73), channel_id=1, source_target_pairs={{0,1},{1,2},{2,3},{4,5},{5,6},{6,7},{8,9},{9,10},{10,11},{12,13},{... | collective-permute-start | bytes 23048 | tf_op jit(solution)/shard_map/ppermute | solution.py:20
  213.6 1.3 copy.74
  214.9 1.9 maximum_maximum_fusion.2
  216.8 1.4 collective-permute-done.19
  218.2 2.0 copy.72
  220.3 1.6 multiply_add_fusion.2
  223.5 40.5 %psum.31 = f32[64,64]{0,1:T(8,128)S(1)} all-reduce(f32[64,64]{0,1:T(8,128)S(1)} %convolution_bitcast_fusion.8), channel_id=1, replica_groups=mesh['gz'=2,'gy'=4,'gx'=4] {'gz','gy','gx'}, use_global_device_ids=true, to_apply=%region_5.9 | all-reduce | flops 4096 | bytes 32768 | tf_op jit(solution)/shard_map/psum | solution.py:122
  264.1 5.8 %cholesky.81 = f32[64,64]{1,0:T(8,128)S(1)} custom-call(f32[64,64]{1,0:T(8,128)S(1)} %fusion.39), custom_call_target="Cholesky" | custom-call | tf_op jit(solution)/shard_map/jit(cholesky)/cholesky | solution.py:92
  271.3 4.9 %custom-call.17 = f32[1,64,64]{1,2,0:T(8,128)S(1)} custom-call(f32[1,64,64]{2,1,0:T(8,128)S(1)} %fusion.35), custom_call_target="InvertDiagBlocksLowerTriangular" | custom-call | tf_op jit(solution)/shard_map/triangular_solve/custom-call.2 | solution.py:94
  (132 shorter events, 32.0 us)
Async XLA Ops:
  0.6 19.7 %copy-start = (f32[64,1,8,128]{3,2,1,0:T(8,128)S(1)}, f32[64,1,8,128]{3,2,1,0:T(8,128)}, u32[]{:S(2)}) copy-start(f32[64,1,8,128]{3,2,1,0:T(8,128)} %param.12) | copy-start | bytes 786436
  1.7 18.6 %collective-permute-start.3 = (f32[64,1,8,128]{3,0,2,1:T(8,128)S(1)}, f32[64,1,8,128]{3,0,2,1:T(8,128)S(1)}, u32[]{:S(2)}, u32[]{:S(2)}) collective-permute-start(f32[64,1,8,128]{3,0,2,1:T(8,128)S(1)} %copy.64), channel_id=1, source_target_pairs={{0,16},{1,17},{2,18},{3,19},{4,20},{5,21},{6,22},{7,23},{8,24},{9,... | collective-permute-start | bytes 786440 | tf_op jit(solution)/shard_map/ppermute | solution.py:20
  6.6 13.8 %collective-permute-start.4 = (f32[64,1,8,128]{3,0,2,1:T(8,128)S(1)}, f32[64,1,8,128]{3,0,2,1:T(8,128)S(1)}, u32[]{:S(2)}, u32[]{:S(2)}) collective-permute-start(f32[64,1,8,128]{3,0,2,1:T(8,128)S(1)} %copy.64), channel_id=1, source_target_pairs={{16,0},{17,1},{18,2},{19,3},{20,4},{21,5},{22,6},{23,7},{24,8},{25... | collective-permute-start | bytes 786440 | tf_op jit(solution)/shard_map/ppermute | solution.py:23
  10.0 15.9 %collective-permute-start = (f32[6,1,8,128]{3,2,1,0:T(8,128)S(1)}, f32[6,1,8,128]{3,2,1,0:T(8,128)S(1)}, u32[]{:S(2)}, u32[]{:S(2)}) collective-permute-start(f32[6,1,8,128]{3,2,1,0:T(8,128)S(1)} %select_add_fusion), channel_id=1, source_target_pairs={{0,16},{1,17},{2,18},{3,19},{4,20},{5,21},{6,22},{7,23},{8,24},{9,... | collective-permute-start | bytes 73736 | tf_op jit(solution)/shard_map/ppermute | solution.py:12
  14.6 11.2 %collective-permute-start.2 = (f32[6,1,8,1]{3,2,1,0:T(8,128)S(1)}, f32[6,1,8,1]{3,2,1,0:T(8,128)S(1)}, u32[]{:S(2)}, u32[]{:S(2)}) collective-permute-start(f32[6,1,8,1]{3,2,1,0:T(8,128)S(1)} %slice.282), channel_id=1, source_target_pairs={{0,1},{1,2},{2,3},{4,5},{5,6},{6,7},{8,9},{9,10},{10,11},{12,13},{... | collective-permute-start | bytes 584 | tf_op jit(solution)/shard_map/ppermute | solution.py:12
  18.1 7.8 %collective-permute-start.1 = (f32[6,1,1,128]{3,2,1,0:T(1,128)S(1)}, f32[6,1,1,128]{3,2,1,0:T(1,128)S(1)}, u32[]{:S(2)}, u32[]{:S(2)}) collective-permute-start(f32[6,1,1,128]{3,2,1,0:T(1,128)S(1)} %slice.281), channel_id=1, source_target_pairs={{0,4},{4,8},{8,12},{1,5},{5,9},{9,13},{2,6},{6,10},{10,14},{3,7},{... | collective-permute-start | bytes 9224 | tf_op jit(solution)/shard_map/ppermute | solution.py:12
  20.4 5.6 %collective-permute-start.5 = (f32[64,3,1,128]{3,0,2,1:T(8,128)S(1)}, f32[64,3,1,128]{3,0,2,1:T(8,128)S(1)}, u32[]{:S(2)}, u32[]{:S(2)}) collective-permute-start(f32[64,3,1,128]{3,0,2,1:T(8,128)S(1)} %get-tuple-element.43), channel_id=1, source_target_pairs={{0,4},{4,8},{8,12},{1,5},{5,9},{9,13},{2,6},{6,10},{10,14},{3,7},{... | collective-permute-start | bytes 294920 | tf_op jit(solution)/shard_map/ppermute | solution.py:20
  24.6 3.2 %collective-permute-start.6 = (f32[64,3,1,128]{3,0,2,1:T(8,128)S(1)}, f32[64,3,1,128]{3,0,2,1:T(8,128)S(1)}, u32[]{:S(2)}, u32[]{:S(2)}) collective-permute-start(f32[64,3,1,128]{3,0,2,1:T(8,128)S(1)} %get-tuple-element.44), channel_id=1, source_target_pairs={{4,0},{8,4},{12,8},{5,1},{9,5},{13,9},{6,2},{10,6},{14,10},{7,3},{... | collective-permute-start | bytes 294920 | tf_op jit(solution)/shard_map/ppermute | solution.py:23
  29.2 5.8 %collective-permute-start.8 = (f32[64,3,10,1]{0,3,2,1:T(1,128)}, f32[64,3,10,1]{0,3,2,1:T(1,128)S(1)}, u32[]{:S(2)}, u32[]{:S(2)}) collective-permute-start(f32[64,3,10,1]{0,3,2,1:T(1,128)} %copy.52), channel_id=1, source_target_pairs={{0,1},{1,2},{2,3},{4,5},{5,6},{6,7},{8,9},{9,10},{10,11},{12,13},{... | collective-permute-start | bytes 23048 | tf_op jit(solution)/shard_map/ppermute | solution.py:20
  33.3 8.8 %copy-start.8 = (f32[2,9,129]{2,1,0:T(8,128)}, f32[2,9,129]{2,1,0:T(8,128)S(1)}, u32[]{:S(2)}) copy-start(f32[2,9,129]{2,1,0:T(8,128)S(1)} %get-tuple-element.45) | copy-start | bytes 27868
  33.3 8.8 %copy-start.11 = (f32[2,9,129]{2,1,0:T(8,128)}, f32[2,9,129]{2,1,0:T(8,128)S(1)}, u32[]{:S(2)}) copy-start(f32[2,9,129]{2,1,0:T(8,128)S(1)} %get-tuple-element.46) | copy-start | bytes 27868
  33.3 43.5 %copy-start.1 = (f32[2,9,129]{2,1,0:T(8,128)}, f32[2,9,129]{2,1,0:T(8,128)S(1)}, u32[]{:S(2)}) copy-start(f32[2,9,129]{2,1,0:T(8,128)S(1)} %get-tuple-element.49) | copy-start | bytes 27868
  33.3 43.5 %copy-start.3 = (f32[2,9,129]{2,1,0:T(8,128)}, f32[2,9,129]{2,1,0:T(8,128)S(1)}, u32[]{:S(2)}) copy-start(f32[2,9,129]{2,1,0:T(8,128)S(1)} %get-tuple-element.50) | copy-start | bytes 27868
  33.6 5.6 %collective-permute-start.7 = (f32[64,3,10,1]{0,3,2,1:T(1,128)S(1)}, f32[64,3,10,1]{0,3,2,1:T(1,128)S(1)}, u32[]{:S(2)}, u32[]{:S(2)}) collective-permute-start(f32[64,3,10,1]{0,3,2,1:T(1,128)S(1)} %copy.50), channel_id=1, source_target_pairs={{1,0},{2,1},{3,2},{5,4},{6,5},{7,6},{9,8},{10,9},{11,10},{13,12},{... | collective-permute-start | bytes 23048 | tf_op jit(solution)/shard_map/ppermute | solution.py:23
  36.3 4.3 %copy-start.17 = (f32[2,9,129]{2,1,0:T(8,128)S(1)}, f32[2,9,129]{2,1,0:T(8,128)}, u32[]{:S(2)}) copy-start(f32[2,9,129]{2,1,0:T(8,128)} %get-tuple-element.48) | copy-start | bytes 27868
  40.6 1.5 copy-start.14
  43.2 10.8 %collective-permute-start.10 = (f32[64,1,8,128]{3,0,2,1:T(8,128)S(1)}, f32[64,1,8,128]{3,0,2,1:T(8,128)S(1)}, u32[]{:S(2)}, u32[]{:S(2)}) collective-permute-start(f32[64,1,8,128]{3,0,2,1:T(8,128)S(1)} %fusion.21), channel_id=1, source_target_pairs={{16,0},{17,1},{18,2},{19,3},{20,4},{21,5},{22,6},{23,7},{24,8},{25... | collective-permute-start | bytes 786440 | tf_op jit(solution)/shard_map/ppermute | solution.py:23
  44.5 11.2 %collective-permute-start.9 = (f32[64,1,8,128]{3,0,2,1:T(8,128)S(1)}, f32[64,1,8,128]{3,0,2,1:T(8,128)S(1)}, u32[]{:S(2)}, u32[]{:S(2)}) collective-permute-start(f32[64,1,8,128]{3,0,2,1:T(8,128)S(1)} %fusion.21), channel_id=1, source_target_pairs={{0,16},{1,17},{2,18},{3,19},{4,20},{5,21},{6,22},{7,23},{8,24},{9,... | collective-permute-start | bytes 786440 | tf_op jit(solution)/shard_map/ppermute | solution.py:20
  55.7 3.5 %collective-permute-start.11 = (f32[64,3,1,128]{3,0,2,1:T(8,128)S(1)}, f32[64,3,1,128]{3,0,2,1:T(8,128)S(1)}, u32[]{:S(2)}, u32[]{:S(2)}) collective-permute-start(f32[64,3,1,128]{3,0,2,1:T(8,128)S(1)} %get-tuple-element.41), channel_id=1, source_target_pairs={{0,4},{4,8},{8,12},{1,5},{5,9},{9,13},{2,6},{6,10},{10,14},{3,7},{... | collective-permute-start | bytes 294920 | tf_op jit(solution)/shard_map/ppermute | solution.py:20
  57.9 3.2 %collective-permute-start.12 = (f32[64,3,1,128]{3,0,2,1:T(8,128)S(1)}, f32[64,3,1,128]{3,0,2,1:T(8,128)S(1)}, u32[]{:S(2)}, u32[]{:S(2)}) collective-permute-start(f32[64,3,1,128]{3,0,2,1:T(8,128)S(1)} %get-tuple-element.42), channel_id=1, source_target_pairs={{4,0},{8,4},{12,8},{5,1},{9,5},{13,9},{6,2},{10,6},{14,10},{7,3},{... | collective-permute-start | bytes 294920 | tf_op jit(solution)/shard_map/ppermute | solution.py:23
  61.8 6.8 %collective-permute-start.14 = (f32[64,3,10,1]{0,3,2,1:T(1,128)S(1)}, f32[64,3,10,1]{0,3,2,1:T(1,128)S(1)}, u32[]{:S(2)}, u32[]{:S(2)}) collective-permute-start(f32[64,3,10,1]{0,3,2,1:T(1,128)S(1)} %copy.56), channel_id=1, source_target_pairs={{0,1},{1,2},{2,3},{4,5},{5,6},{6,7},{8,9},{9,10},{10,11},{12,13},{... | collective-permute-start | bytes 23048 | tf_op jit(solution)/shard_map/ppermute | solution.py:20
  67.3 5.9 %collective-permute-start.13 = (f32[64,3,10,1]{0,3,2,1:T(1,128)}, f32[64,3,10,1]{0,3,2,1:T(1,128)}, u32[]{:S(2)}, u32[]{:S(2)}) collective-permute-start(f32[64,3,10,1]{0,3,2,1:T(1,128)} %copy.54), channel_id=1, source_target_pairs={{1,0},{2,1},{3,2},{5,4},{6,5},{7,6},{9,8},{10,9},{11,10},{13,12},{... | collective-permute-start | bytes 23048 | tf_op jit(solution)/shard_map/ppermute | solution.py:23
  75.3 1.5 copy-start.9
  75.3 1.5 copy-start.12
  75.3 1.5 copy-start.15
  77.5 1.0 copy-start.22
  146.0 40.7 %copy-start.18 = (f32[64,64,1]{0,1,2:T(8,128)}, f32[64,64,1]{0,1,2:T(8,128)S(1)}, u32[]{:S(2)}) copy-start(f32[64,64,1]{0,1,2:T(8,128)S(1)} %convolution_bitcast_fusion.7) | copy-start | bytes 49156
  185.6 0.6 copy-start.20
  186.6 9.4 %collective-permute-start.15 = (f32[64,1,8,128]{3,0,2,1:T(8,128)S(1)}, f32[64,1,8,128]{3,0,2,1:T(8,128)S(1)}, u32[]{:S(2)}, u32[]{:S(2)}) collective-permute-start(f32[64,1,8,128]{3,0,2,1:T(8,128)S(1)} %fusion.6), channel_id=1, source_target_pairs={{0,16},{1,17},{2,18},{3,19},{4,20},{5,21},{6,22},{7,23},{8,24},{9,... | collective-permute-start | bytes 786440 | tf_op jit(solution)/shard_map/ppermute | solution.py:20
  190.9 9.3 %collective-permute-start.16 = (f32[64,1,8,128]{3,0,2,1:T(8,128)S(1)}, f32[64,1,8,128]{3,0,2,1:T(8,128)S(1)}, u32[]{:S(2)}, u32[]{:S(2)}) collective-permute-start(f32[64,1,8,128]{3,0,2,1:T(8,128)S(1)} %fusion.6), channel_id=1, source_target_pairs={{16,0},{17,1},{18,2},{19,3},{20,4},{21,5},{22,6},{23,7},{24,8},{25... | collective-permute-start | bytes 786440 | tf_op jit(solution)/shard_map/ppermute | solution.py:23
  200.2 2.6 collective-permute-start.17
  201.5 4.3 %collective-permute-start.18 = (f32[64,3,1,128]{3,0,2,1:T(8,128)S(1)}, f32[64,3,1,128]{3,0,2,1:T(8,128)S(1)}, u32[]{:S(2)}, u32[]{:S(2)}) collective-permute-start(f32[64,3,1,128]{3,0,2,1:T(8,128)S(1)} %get-tuple-element.40), channel_id=1, source_target_pairs={{4,0},{8,4},{12,8},{5,1},{9,5},{13,9},{6,2},{10,6},{14,10},{7,3},{... | collective-permute-start | bytes 294920 | tf_op jit(solution)/shard_map/ppermute | solution.py:23
  202.8 2.9 %copy-start.6 = (f32[64,3,1,128]{3,0,2,1:T(8,128)}, f32[64,3,1,128]{3,0,2,1:T(8,128)S(1)}, u32[]{:S(2)}) copy-start(f32[64,3,1,128]{3,0,2,1:T(8,128)S(1)} %collective-permute-done.17) | copy-start | bytes 294916
  205.7 0.6 copy-start.7
  207.2 6.4 %collective-permute-start.20 = (f32[64,3,10,1]{0,3,2,1:T(1,128)S(1)}, f32[64,3,10,1]{0,3,2,1:T(1,128)S(1)}, u32[]{:S(2)}, u32[]{:S(2)}) collective-permute-start(f32[64,3,10,1]{0,3,2,1:T(1,128)S(1)} %copy.73), channel_id=1, source_target_pairs={{0,1},{1,2},{2,3},{4,5},{5,6},{6,7},{8,9},{9,10},{10,11},{12,13},{... | collective-permute-start | bytes 23048 | tf_op jit(solution)/shard_map/ppermute | solution.py:20
  212.3 5.9 %collective-permute-start.19 = (f32[64,3,10,1]{0,3,2,1:T(1,128)}, f32[64,3,10,1]{0,3,2,1:T(1,128)}, u32[]{:S(2)}, u32[]{:S(2)}) collective-permute-start(f32[64,3,10,1]{0,3,2,1:T(1,128)} %copy.71), channel_id=1, source_target_pairs={{1,0},{2,1},{3,2},{5,4},{6,5},{7,6},{9,8},{10,9},{11,10},{13,12},{... | collective-permute-start | bytes 23048 | tf_op jit(solution)/shard_map/ppermute | solution.py:23
  220.3 1.6 copy-start.2
  220.3 1.6 copy-start.4
  220.3 1.6 copy-start.10
  220.3 1.6 copy-start.13
  220.3 1.6 copy-start.16
  222.6 53.6 %copy-start.21 = (f32[64,64]{1,0:T(8,128)S(1)}, f32[64,64]{1,0:T(8,128)}, u32[]{:S(2)}) copy-start(f32[64,64]{1,0:T(8,128)} %copy-done.20) | copy-start | bytes 49156
  223.4 54.6 %copy-start.5 = (f32[64,1,8,128]{3,2,0,1:T(8,128)S(1)}, f32[64,1,8,128]{3,2,0,1:T(8,128)}, u32[]{:S(2)}) copy-start(f32[64,1,8,128]{3,2,0,1:T(8,128)} %copy.77) | copy-start | bytes 786436
  264.0 14.4 %copy-start.19 = (f32[64,64,1]{0,1,2:T(8,128)S(1)}, f32[64,64,1]{0,1,2:T(8,128)}, u32[]{:S(2)}) copy-start(f32[64,64,1]{0,1,2:T(8,128)} %copy-done.18) | copy-start | bytes 49156
where the time goes:
time: 281 us; the launch traced here: 280 us
  blocking collectives  122 us (43%)
  starting transfers between devices  52.4 us (19%)
  other arithmetic  50.7 us (18%)
  waiting for transfers between devices  25.3 us (9%)
  local copies, waits for them, and re-layouts  22.4 us (8%)
  matrix products  5.49 us (2%)
    psum x1, blocking collectives, body(): rr_now = lax.psum(gram_of(residual, residual), ('gz', 'gy', 'gx'))  42.6 us
    psum x1, blocking collectives, body(): curve = lax.psum(gram_of(direction, image), ('gz', 'gy', 'gx'))  40.5 us
    psum x1, blocking collectives, body(): rr_next = lax.psum(gram_of(residual, residual), ('gz', 'gy', 'gx'))  38.9 us
    ppermute x9, starting transfers between devices, padded_2(): lax.ppermute(lax.slice_in_dim(block, block.shape[dim] - width, None, axis...  31.5 us
    ppermute x9, waiting for transfers between devices, padded_2(): lax.ppermute(lax.slice_in_dim(block, 0, width, axis=dim), axis, backward)  19.7 us
    another operation x9, other arithmetic, factor_solve(): factor = jnp.linalg.cholesky(matrix)  19.6 us
    another operation x6, other arithmetic, factor_solve(): lax.linalg.triangular_solve(factor, halfway, left_side=True, lower=True,...  16.6 us
    ppermute x9, starting transfers between devices, padded_2(): lax.ppermute(lax.slice_in_dim(block, 0, width, axis=dim), axis, backward)  11.6 us
  transfers between devices with their start and end apart: 21, of which 10 were waited for; matrix products, arithmetic and copies ran while one was open for 6% of the time, Pallas kernels for 0%

commit v1 on v0

--- a/solution.py
+++ b/solution.py
@@ -116,7 +116,7 @@
     solution = initial
     residual = sources - operate(initial)
     direction = residual
-    rr_now = lax.psum(gram_of(residual, residual), ("gz", "gy", "gx"))
+    rr_now = jnp.sum(lax.all_gather(gram_of(residual, residual), ("gz", "gy", "gx")), axis=0)
     for iteration in range(ITERS):
         image = operate(direction)
         curve = lax.psum(gram_of(direction, image), ("gz", "gy", "gx"))

time: 281 us -> 343 us (1.22)
  blocking collectives: 122 us -> 194 us
  waiting for transfers between devices: 25.3 us -> 17.5 us
    all_gather x0 -> x1, blocking collectives: none -> 74.6 us  [body(): lax.all_gather(gram_of(residual, residual), ('gz', 'gy', 'gx'))]
    psum x1 -> x0, blocking collectives: 42.6 us -> none  [body(): rr_now = lax.psum(gram_of(residual, residual), ('gz', 'gy', 'gx'))]
    psum x1 -> x2, blocking collectives: 40.5 us -> 79.6 us  [body(): curve = lax.psum(gram_of(direction, image), ('gz', 'gy', 'gx'))]
    ppermute x9, waiting for transfers between devices: 19.7 us -> 14.2 us  [padded_2(): lax.ppermute(lax.slice_in_dim(block, 0, width, axis=dim), axis, backward)]
  transfers between devices with their start and end apart: 21 -> 21, of which waited for: 10 -> 8; matrix products, arithmetic and copies ran while one was open for 6% -> 9% of each run, Pallas kernels for 0% -> 0%
where the time goes in v1:
time: 343 us; the launch traced here: 341 us
  blocking collectives  194 us (57%)
  other arithmetic  51.5 us (15%)
  starting transfers between devices  49.7 us (14%)
  local copies, waits for them, and re-layouts  22.4 us (7%)
  waiting for transfers between devices  17.5 us (5%)
  matrix products  4.85 us (1%)
    psum x2, blocking collectives, body(): curve = lax.psum(gram_of(direction, image), ('gz', 'gy', 'gx'))  79.6 us
    all_gather x1, blocking collectives, body(): lax.all_gather(gram_of(residual, residual), ('gz', 'gy', 'gx'))  74.6 us
    psum x1, blocking collectives, body(): rr_next = lax.psum(gram_of(residual, residual), ('gz', 'gy', 'gx'))  39.8 us
    ppermute x9, starting transfers between devices, padded_2(): lax.ppermute(lax.slice_in_dim(block, block.shape[dim] - width, None, axis...  28.8 us
    another operation x9, other arithmetic, factor_solve(): factor = jnp.linalg.cholesky(matrix)  19.6 us
    another operation x6, other arithmetic, factor_solve(): lax.linalg.triangular_solve(factor, halfway, left_side=True, lower=True,...  17.3 us
    ppermute x9, waiting for transfers between devices, padded_2(): lax.ppermute(lax.slice_in_dim(block, 0, width, axis=dim), axis, backward)  14.2 us
    ppermute x9, starting transfers between devices, padded_2(): lax.ppermute(lax.slice_in_dim(block, 0, width, axis=dim), axis, backward)  11.6 us
  transfers between devices with their start and end apart: 21, of which 8 were waited for; matrix products, arithmetic and copies ran while one was open for 9% of the time, Pallas kernels for 0%

profile of v1, /device:TPU:0, one launch (start us, length us, event | category | flops | bytes accessed | tf_op | source)
XLA Modules:
  0.0 341.4 jit_solution(13187715406471645363)
XLA Ops:
  1.7 4.9 %collective-permute-start.3 = (f32[64,1,8,128]{3,0,2,1:T(8,128)S(1)}, f32[64,1,8,128]{3,0,2,1:T(8,128)S(1)}, u32[]{:S(2)}, u32[]{:S(2)}) collective-permute-start(f32[64,1,8,128]{3,0,2,1:T(8,128)S(1)} %copy.61), channel_id=1, source_target_pairs={{0,16},{1,17},{2,18},{3,19},{4,20},{5,21},{6,22},{7,23},{8,24},{9,... | collective-permute-start | bytes 786440 | tf_op jit(solution)/shard_map/ppermute | solution.py:20
  6.6 1.3 collective-permute-start.4
  10.0 4.6 %collective-permute-start = (f32[6,1,8,128]{3,2,1,0:T(8,128)S(1)}, f32[6,1,8,128]{3,2,1,0:T(8,128)S(1)}, u32[]{:S(2)}, u32[]{:S(2)}) collective-permute-start(f32[6,1,8,128]{3,2,1,0:T(8,128)S(1)} %select_add_fusion), channel_id=1, source_target_pairs={{0,16},{1,17},{2,18},{3,19},{4,20},{5,21},{6,22},{7,23},{8,24},{9,... | collective-permute-start | bytes 73736 | tf_op jit(solution)/shard_map/ppermute | solution.py:12
  14.6 3.5 %collective-permute-start.2 = (f32[6,1,8,1]{3,2,1,0:T(8,128)S(1)}, f32[6,1,8,1]{3,2,1,0:T(8,128)S(1)}, u32[]{:S(2)}, u32[]{:S(2)}) collective-permute-start(f32[6,1,8,1]{3,2,1,0:T(8,128)S(1)} %slice.282), channel_id=1, source_target_pairs={{0,1},{1,2},{2,3},{4,5},{5,6},{6,7},{8,9},{9,10},{10,11},{12,13},{... | collective-permute-start | bytes 584 | tf_op jit(solution)/shard_map/ppermute | solution.py:12
  18.1 1.3 collective-permute-start.1
  20.4 4.1 %collective-permute-start.5 = (f32[64,3,1,128]{3,0,2,1:T(8,128)S(1)}, f32[64,3,1,128]{3,0,2,1:T(8,128)S(1)}, u32[]{:S(2)}, u32[]{:S(2)}) collective-permute-start(f32[64,3,1,128]{3,0,2,1:T(8,128)S(1)} %get-tuple-element.41), channel_id=1, source_target_pairs={{0,4},{4,8},{8,12},{1,5},{5,9},{9,13},{2,6},{6,10},{10,14},{3,7},{... | collective-permute-start | bytes 294920 | tf_op jit(solution)/shard_map/ppermute | solution.py:20
  24.6 1.3 collective-permute-start.6
  26.1 1.7 collective-permute-done.6
  29.2 3.5 %collective-permute-start.8 = (f32[64,3,10,1]{0,3,2,1:T(1,128)}, f32[64,3,10,1]{0,3,2,1:T(1,128)S(1)}, u32[]{:S(2)}, u32[]{:S(2)}) collective-permute-start(f32[64,3,10,1]{0,3,2,1:T(1,128)} %copy.50), channel_id=1, source_target_pairs={{0,1},{1,2},{2,3},{4,5},{5,6},{6,7},{8,9},{9,10},{10,11},{12,13},{... | collective-permute-start | bytes 23048 | tf_op jit(solution)/shard_map/ppermute | solution.py:20
  33.6 1.3 collective-permute-start.7
  35.0 1.3 copy.51
  36.3 1.8 maximum_maximum_fusion
  39.3 1.3 copy.49
  40.6 1.5 multiply_add_fusion.8
  43.6 1.3 collective-permute-start.10
  44.9 4.6 %collective-permute-start.9 = (f32[64,1,8,128]{3,0,2,1:T(8,128)S(1)}, f32[64,1,8,128]{3,0,2,1:T(8,128)S(1)}, u32[]{:S(2)}, u32[]{:S(2)}) collective-permute-start(f32[64,1,8,128]{3,0,2,1:T(8,128)S(1)} %fusion.21), channel_id=1, source_target_pairs={{0,16},{1,17},{2,18},{3,19},{4,20},{5,21},{6,22},{7,23},{8,24},{9,... | collective-permute-start | bytes 786440 | tf_op jit(solution)/shard_map/ppermute | solution.py:20
  49.5 74.6 %all-gather = f32[2048,64]{1,0:T(8,128)S(1)} all-gather(f32[64,64]{1,0:T(8,128)S(1)} %convolution_bitcast_fusion.10), channel_id=2, replica_groups=mesh['gz'=2,'gy'=4,'gx'=4] {'gz','gy','gx'}, dimensions={0}, use_global_device_ids=true | all-gather | bytes 540672 | tf_op jit(solution)/shard_map/all_gather | solution.py:119
  124.2 5.8 %cholesky.70 = f32[64,64]{1,0:T(8,128)S(1)} custom-call(f32[64,64]{1,0:T(8,128)S(1)} %fusion.43), custom_call_target="Cholesky" | custom-call | tf_op jit(solution)/shard_map/jit(cholesky)/cholesky | solution.py:92
  130.1 1.3 collective-permute-start.11
  131.4 1.3 collective-permute-start.12
  135.4 1.9 collective-permute-start.14
  138.2 5.5 %custom-call.15 = f32[1,64,64]{1,2,0:T(8,128)} custom-call(f32[1,64,64]{2,1,0:T(8,128)S(1)} %fusion.34), custom_call_target="InvertDiagBlocksLowerTriangular" | custom-call | tf_op jit(solution)/shard_map/triangular_solve/custom-call.2 | solution.py:94
  144.6 1.3 collective-permute-start.13
  145.9 1.3 copy.55
  147.3 1.8 maximum_maximum_fusion.1
  149.0 1.5 collective-permute-done.13
  150.6 2.0 copy.53
  152.6 1.5 multiply_add_fusion.5
  155.8 39.2 %psum.21 = f32[64,64]{0,1:T(8,128)S(1)} all-reduce(f32[64,64]{0,1:T(8,128)S(1)} %convolution_bitcast_fusion.11), channel_id=1, replica_groups=mesh['gz'=2,'gy'=4,'gx'=4] {'gz','gy','gx'}, use_global_device_ids=true, to_apply=%region_0.1 | all-reduce | flops 4096 | bytes 32768 | tf_op jit(solution)/shard_map/psum | solution.py:122
  195.1 5.8 %cholesky.59 = f32[64,64]{1,0:T(8,128)S(1)} custom-call(f32[64,64]{1,0:T(8,128)S(1)} %fusion.47), custom_call_target="Cholesky" | custom-call | tf_op jit(solution)/shard_map/jit(cholesky)/cholesky | solution.py:92
  202.4 4.9 %custom-call.13 = f32[1,64,64]{1,2,0:T(8,128)S(1)} custom-call(f32[1,64,64]{2,1,0:T(8,128)S(1)} %fusion.33), custom_call_target="InvertDiagBlocksLowerTriangular" | custom-call | tf_op jit(solution)/shard_map/triangular_solve/custom-call.2 | solution.py:94
  208.5 39.8 %psum.22 = f32[64,64]{1,0:T(8,128)S(1)} all-reduce(f32[64,64]{1,0:T(8,128)S(1)} %convolution_bitcast_fusion.9), channel_id=1, replica_groups=mesh['gz'=2,'gy'=4,'gx'=4] {'gz','gy','gx'}, use_global_device_ids=true, to_apply=%region_4.8 | all-reduce | flops 4096 | bytes 32768 | tf_op jit(solution)/shard_map/psum | solution.py:127
  249.3 4.2 %collective-permute-start.15 = (f32[64,1,8,128]{3,0,2,1:T(8,128)S(1)}, f32[64,1,8,128]{3,0,2,1:T(8,128)S(1)}, u32[]{:S(2)}, u32[]{:S(2)}) collective-permute-start(f32[64,1,8,128]{3,0,2,1:T(8,128)S(1)} %fusion.6), channel_id=1, source_target_pairs={{0,16},{1,17},{2,18},{3,19},{4,20},{5,21},{6,22},{7,23},{8,24},{9,... | collective-permute-start | bytes 786440 | tf_op jit(solution)/shard_map/ppermute | solution.py:20
  253.6 1.3 collective-permute-start.16
  254.9 3.3 collective-permute-done.15
  258.2 4.1 %collective-permute-done.16 = f32[64,1,8,128]{3,0,2,1:T(8,128)S(1)} collective-permute-done((f32[64,1,8,128]{3,0,2,1:T(8,128)S(1)}, f32[64,1,8,128]{3,0,2,1:T(8,128)S(1)}, u32[]{:S(2)}, u32[]{:S(2)}) %collective-permute-start.16) | collective-permute-done | bytes 262176 | tf_op jit(solution)/shard_map/ppermute | solution.py:23
  262.3 1.3 collective-permute-start.17
  263.6 1.3 collective-permute-start.18
  264.9 2.9 collective-permute-done.18
  269.3 3.0 collective-permute-start.20
  275.4 1.3 copy.71
  276.8 1.9 maximum_maximum_fusion.2
  278.6 1.4 collective-permute-done.19
  280.1 2.0 copy.69
  282.1 1.6 multiply_add_fusion.2
  285.4 40.4 %psum.23 = f32[64,64]{0,1:T(8,128)S(1)} all-reduce(f32[64,64]{0,1:T(8,128)S(1)} %convolution_bitcast_fusion.8), channel_id=1, replica_groups=mesh['gz'=2,'gy'=4,'gx'=4] {'gz','gy','gx'}, use_global_device_ids=true, to_apply=%region_5.9 | all-reduce | flops 4096 | bytes 32768 | tf_op jit(solution)/shard_map/psum | solution.py:122
  325.9 5.8 %cholesky.81 = f32[64,64]{1,0:T(8,128)S(1)} custom-call(f32[64,64]{1,0:T(8,128)S(1)} %fusion.39), custom_call_target="Cholesky" | custom-call | tf_op jit(solution)/shard_map/jit(cholesky)/cholesky | solution.py:92
  333.1 4.9 %custom-call.17 = f32[1,64,64]{1,2,0:T(8,128)S(1)} custom-call(f32[1,64,64]{2,1,0:T(8,128)S(1)} %fusion.35), custom_call_target="InvertDiagBlocksLowerTriangular" | custom-call | tf_op jit(solution)/shard_map/triangular_solve/custom-call.2 | solution.py:94
  (139 shorter events, 30.3 us)
Async XLA Ops:
  0.6 19.7 %copy-start = (f32[64,1,8,128]{3,2,1,0:T(8,128)S(1)}, f32[64,1,8,128]{3,2,1,0:T(8,128)}, u32[]{:S(2)}) copy-start(f32[64,1,8,128]{3,2,1,0:T(8,128)} %param.12) | copy-start | bytes 786436
  1.7 18.6 %collective-permute-start.3 = (f32[64,1,8,128]{3,0,2,1:T(8,128)S(1)}, f32[64,1,8,128]{3,0,2,1:T(8,128)S(1)}, u32[]{:S(2)}, u32[]{:S(2)}) collective-permute-start(f32[64,1,8,128]{3,0,2,1:T(8,128)S(1)} %copy.61), channel_id=1, source_target_pairs={{0,16},{1,17},{2,18},{3,19},{4,20},{5,21},{6,22},{7,23},{8,24},{9,... | collective-permute-start | bytes 786440 | tf_op jit(solution)/shard_map/ppermute | solution.py:20
  6.6 13.8 %collective-permute-start.4 = (f32[64,1,8,128]{3,0,2,1:T(8,128)S(1)}, f32[64,1,8,128]{3,0,2,1:T(8,128)S(1)}, u32[]{:S(2)}, u32[]{:S(2)}) collective-permute-start(f32[64,1,8,128]{3,0,2,1:T(8,128)S(1)} %copy.61), channel_id=1, source_target_pairs={{16,0},{17,1},{18,2},{19,3},{20,4},{21,5},{22,6},{23,7},{24,8},{25... | collective-permute-start | bytes 786440 | tf_op jit(solution)/shard_map/ppermute | solution.py:23
  10.0 15.9 %collective-permute-start = (f32[6,1,8,128]{3,2,1,0:T(8,128)S(1)}, f32[6,1,8,128]{3,2,1,0:T(8,128)S(1)}, u32[]{:S(2)}, u32[]{:S(2)}) collective-permute-start(f32[6,1,8,128]{3,2,1,0:T(8,128)S(1)} %select_add_fusion), channel_id=1, source_target_pairs={{0,16},{1,17},{2,18},{3,19},{4,20},{5,21},{6,22},{7,23},{8,24},{9,... | collective-permute-start | bytes 73736 | tf_op jit(solution)/shard_map/ppermute | solution.py:12
  14.6 11.2 %collective-permute-start.2 = (f32[6,1,8,1]{3,2,1,0:T(8,128)S(1)}, f32[6,1,8,1]{3,2,1,0:T(8,128)S(1)}, u32[]{:S(2)}, u32[]{:S(2)}) collective-permute-start(f32[6,1,8,1]{3,2,1,0:T(8,128)S(1)} %slice.282), channel_id=1, source_target_pairs={{0,1},{1,2},{2,3},{4,5},{5,6},{6,7},{8,9},{9,10},{10,11},{12,13},{... | collective-permute-start | bytes 584 | tf_op jit(solution)/shard_map/ppermute | solution.py:12
  18.1 7.8 %collective-permute-start.1 = (f32[6,1,1,128]{3,2,1,0:T(1,128)S(1)}, f32[6,1,1,128]{3,2,1,0:T(1,128)S(1)}, u32[]{:S(2)}, u32[]{:S(2)}) collective-permute-start(f32[6,1,1,128]{3,2,1,0:T(1,128)S(1)} %slice.281), channel_id=1, source_target_pairs={{0,4},{4,8},{8,12},{1,5},{5,9},{9,13},{2,6},{6,10},{10,14},{3,7},{... | collective-permute-start | bytes 9224 | tf_op jit(solution)/shard_map/ppermute | solution.py:12
  20.4 5.6 %collective-permute-start.5 = (f32[64,3,1,128]{3,0,2,1:T(8,128)S(1)}, f32[64,3,1,128]{3,0,2,1:T(8,128)S(1)}, u32[]{:S(2)}, u32[]{:S(2)}) collective-permute-start(f32[64,3,1,128]{3,0,2,1:T(8,128)S(1)} %get-tuple-element.41), channel_id=1, source_target_pairs={{0,4},{4,8},{8,12},{1,5},{5,9},{9,13},{2,6},{6,10},{10,14},{3,7},{... | collective-permute-start | bytes 294920 | tf_op jit(solution)/shard_map/ppermute | solution.py:20
  24.6 3.2 collective-permute-start.6
  29.2 5.8 %collective-permute-start.8 = (f32[64,3,10,1]{0,3,2,1:T(1,128)}, f32[64,3,10,1]{0,3,2,1:T(1,128)S(1)}, u32[]{:S(2)}, u32[]{:S(2)}) collective-permute-start(f32[64,3,10,1]{0,3,2,1:T(1,128)} %copy.50), channel_id=1, source_target_pairs={{0,1},{1,2},{2,3},{4,5},{5,6},{6,7},{8,9},{9,10},{10,11},{12,13},{... | collective-permute-start | bytes 23048 | tf_op jit(solution)/shard_map/ppermute | solution.py:20
  33.3 8.8 %copy-start.8 = (f32[2,9,129]{2,1,0:T(8,128)}, f32[2,9,129]{2,1,0:T(8,128)S(1)}, u32[]{:S(2)}) copy-start(f32[2,9,129]{2,1,0:T(8,128)S(1)} %get-tuple-element.43) | copy-start | bytes 27868
  33.3 8.8 %copy-start.11 = (f32[2,9,129]{2,1,0:T(8,128)}, f32[2,9,129]{2,1,0:T(8,128)S(1)}, u32[]{:S(2)}) copy-start(f32[2,9,129]{2,1,0:T(8,128)S(1)} %get-tuple-element.44) | copy-start | bytes 27868
  33.3 120.8 %copy-start.1 = (f32[2,9,129]{2,1,0:T(8,128)}, f32[2,9,129]{2,1,0:T(8,128)S(1)}, u32[]{:S(2)}) copy-start(f32[2,9,129]{2,1,0:T(8,128)S(1)} %get-tuple-element.47) | copy-start | bytes 27868
  33.3 120.8 %copy-start.3 = (f32[2,9,129]{2,1,0:T(8,128)}, f32[2,9,129]{2,1,0:T(8,128)S(1)}, u32[]{:S(2)}) copy-start(f32[2,9,129]{2,1,0:T(8,128)S(1)} %get-tuple-element.48) | copy-start | bytes 27868
  33.6 5.6 %collective-permute-start.7 = (f32[64,3,10,1]{0,3,2,1:T(1,128)S(1)}, f32[64,3,10,1]{0,3,2,1:T(1,128)S(1)}, u32[]{:S(2)}, u32[]{:S(2)}) collective-permute-start(f32[64,3,10,1]{0,3,2,1:T(1,128)S(1)} %copy.48), channel_id=1, source_target_pairs={{1,0},{2,1},{3,2},{5,4},{6,5},{7,6},{9,8},{10,9},{11,10},{13,12},{... | collective-permute-start | bytes 23048 | tf_op jit(solution)/shard_map/ppermute | solution.py:23
  36.3 4.3 %copy-start.17 = (f32[2,9,129]{2,1,0:T(8,128)S(1)}, f32[2,9,129]{2,1,0:T(8,128)}, u32[]{:S(2)}) copy-start(f32[2,9,129]{2,1,0:T(8,128)} %get-tuple-element.46) | copy-start | bytes 27868
  40.6 1.5 copy-start.14
  43.6 86.5 %collective-permute-start.10 = (f32[64,1,8,128]{3,0,2,1:T(8,128)S(1)}, f32[64,1,8,128]{3,0,2,1:T(8,128)S(1)}, u32[]{:S(2)}, u32[]{:S(2)}) collective-permute-start(f32[64,1,8,128]{3,0,2,1:T(8,128)S(1)} %fusion.21), channel_id=1, source_target_pairs={{16,0},{17,1},{18,2},{19,3},{20,4},{21,5},{22,6},{23,7},{24,8},{25... | collective-permute-start | bytes 786440 | tf_op jit(solution)/shard_map/ppermute | solution.py:23
  44.9 85.2 %collective-permute-start.9 = (f32[64,1,8,128]{3,0,2,1:T(8,128)S(1)}, f32[64,1,8,128]{3,0,2,1:T(8,128)S(1)}, u32[]{:S(2)}, u32[]{:S(2)}) collective-permute-start(f32[64,1,8,128]{3,0,2,1:T(8,128)S(1)} %fusion.21), channel_id=1, source_target_pairs={{0,16},{1,17},{2,18},{3,19},{4,20},{5,21},{6,22},{7,23},{8,24},{9,... | collective-permute-start | bytes 786440 | tf_op jit(solution)/shard_map/ppermute | solution.py:20
  124.1 6.0 %copy-start.18 = (f32[64,64]{1,0:T(8,128)}, f32[64,64]{1,0:T(8,128)S(1)}, u32[]{:S(2)}) copy-start(f32[64,64]{1,0:T(8,128)S(1)} %reduce_sum.9) | copy-start | bytes 49156
  130.1 3.2 collective-permute-start.11
  131.4 3.2 collective-permute-start.12
  135.4 10.5 %collective-permute-start.14 = (f32[64,3,10,1]{0,3,2,1:T(1,128)S(1)}, f32[64,3,10,1]{0,3,2,1:T(1,128)S(1)}, u32[]{:S(2)}, u32[]{:S(2)}) collective-permute-start(f32[64,3,10,1]{0,3,2,1:T(1,128)S(1)} %copy.54), channel_id=1, source_target_pairs={{0,1},{1,2},{2,3},{4,5},{5,6},{6,7},{8,9},{9,10},{10,11},{12,13},{... | collective-permute-start | bytes 23048 | tf_op jit(solution)/shard_map/ppermute | solution.py:20
  144.6 5.9 %collective-permute-start.13 = (f32[64,3,10,1]{0,3,2,1:T(1,128)}, f32[64,3,10,1]{0,3,2,1:T(1,128)}, u32[]{:S(2)}, u32[]{:S(2)}) collective-permute-start(f32[64,3,10,1]{0,3,2,1:T(1,128)} %copy.52), channel_id=1, source_target_pairs={{1,0},{2,1},{3,2},{5,4},{6,5},{7,6},{9,8},{10,9},{11,10},{13,12},{... | collective-permute-start | bytes 23048 | tf_op jit(solution)/shard_map/ppermute | solution.py:23
  152.6 1.5 copy-start.9
  152.6 1.5 copy-start.12
  152.6 1.5 copy-start.15
  154.8 52.4 %copy-start.19 = (f32[64,64]{1,0:T(8,128)S(1)}, f32[64,64]{1,0:T(8,128)}, u32[]{:S(2)}) copy-start(f32[64,64]{1,0:T(8,128)} %copy-done.18) | copy-start | bytes 49156
  155.6 92.7 %copy-start.24 = (f32[1,64,64]{1,2,0:T(8,128)S(1)}, f32[1,64,64]{1,2,0:T(8,128)}, u32[]{:S(2)}) copy-start(f32[1,64,64]{1,2,0:T(8,128)} %custom-call.15) | copy-start | bytes 49156
  207.8 41.6 %copy-start.20 = (f32[64,64,1]{0,1,2:T(8,128)}, f32[64,64,1]{0,1,2:T(8,128)S(1)}, u32[]{:S(2)}) copy-start(f32[64,64,1]{0,1,2:T(8,128)S(1)} %convolution_bitcast_fusion.7) | copy-start | bytes 49156
  248.3 0.6 copy-start.22
  249.3 8.8 %collective-permute-start.15 = (f32[64,1,8,128]{3,0,2,1:T(8,128)S(1)}, f32[64,1,8,128]{3,0,2,1:T(8,128)S(1)}, u32[]{:S(2)}, u32[]{:S(2)}) collective-permute-start(f32[64,1,8,128]{3,0,2,1:T(8,128)S(1)} %fusion.6), channel_id=1, source_target_pairs={{0,16},{1,17},{2,18},{3,19},{4,20},{5,21},{6,22},{7,23},{8,24},{9,... | collective-permute-start | bytes 786440 | tf_op jit(solution)/shard_map/ppermute | solution.py:20
  253.6 8.7 %collective-permute-start.16 = (f32[64,1,8,128]{3,0,2,1:T(8,128)S(1)}, f32[64,1,8,128]{3,0,2,1:T(8,128)S(1)}, u32[]{:S(2)}, u32[]{:S(2)}) collective-permute-start(f32[64,1,8,128]{3,0,2,1:T(8,128)S(1)} %fusion.6), channel_id=1, source_target_pairs={{16,0},{17,1},{18,2},{19,3},{20,4},{21,5},{22,6},{23,7},{24,8},{25... | collective-permute-start | bytes 786440 | tf_op jit(solution)/shard_map/ppermute | solution.py:23
  262.3 2.6 collective-permute-start.17
  263.6 4.3 %collective-permute-start.18 = (f32[64,3,1,128]{3,0,2,1:T(8,128)S(1)}, f32[64,3,1,128]{3,0,2,1:T(8,128)S(1)}, u32[]{:S(2)}, u32[]{:S(2)}) collective-permute-start(f32[64,3,1,128]{3,0,2,1:T(8,128)S(1)} %get-tuple-element.38), channel_id=1, source_target_pairs={{4,0},{8,4},{12,8},{5,1},{9,5},{13,9},{6,2},{10,6},{14,10},{7,3},{... | collective-permute-start | bytes 294920 | tf_op jit(solution)/shard_map/ppermute | solution.py:23
  264.9 2.9 copy-start.6
  267.9 0.6 copy-start.7
  269.3 6.2 %collective-permute-start.20 = (f32[64,3,10,1]{0,3,2,1:T(1,128)S(1)}, f32[64,3,10,1]{0,3,2,1:T(1,128)S(1)}, u32[]{:S(2)}, u32[]{:S(2)}) collective-permute-start(f32[64,3,10,1]{0,3,2,1:T(1,128)S(1)} %copy.70), channel_id=1, source_target_pairs={{0,1},{1,2},{2,3},{4,5},{5,6},{6,7},{8,9},{9,10},{10,11},{12,13},{... | collective-permute-start | bytes 23048 | tf_op jit(solution)/shard_map/ppermute | solution.py:20
  274.1 5.9 %collective-permute-start.19 = (f32[64,3,10,1]{0,3,2,1:T(1,128)}, f32[64,3,10,1]{0,3,2,1:T(1,128)}, u32[]{:S(2)}, u32[]{:S(2)}) collective-permute-start(f32[64,3,10,1]{0,3,2,1:T(1,128)} %copy.68), channel_id=1, source_target_pairs={{1,0},{2,1},{3,2},{5,4},{6,5},{7,6},{9,8},{10,9},{11,10},{13,12},{... | collective-permute-start | bytes 23048 | tf_op jit(solution)/shard_map/ppermute | solution.py:23
  282.1 1.6 copy-start.2
  282.1 1.6 copy-start.4
  282.1 1.6 copy-start.10
  282.1 1.6 copy-start.13
  282.1 1.6 copy-start.16
  284.4 53.6 %copy-start.23 = (f32[64,64]{1,0:T(8,128)S(1)}, f32[64,64]{1,0:T(8,128)}, u32[]{:S(2)}) copy-start(f32[64,64]{1,0:T(8,128)} %copy-done.22) | copy-start | bytes 49156
  285.2 54.6 %copy-start.5 = (f32[64,1,8,128]{3,2,0,1:T(8,128)S(1)}, f32[64,1,8,128]{3,2,0,1:T(8,128)}, u32[]{:S(2)}) copy-start(f32[64,1,8,128]{3,2,0,1:T(8,128)} %copy.74) | copy-start | bytes 786436
  325.8 14.4 %copy-start.21 = (f32[64,64,1]{0,1,2:T(8,128)S(1)}, f32[64,64,1]{0,1,2:T(8,128)}, u32[]{:S(2)}) copy-start(f32[64,64,1]{0,1,2:T(8,128)} %copy-done.20) | copy-start | bytes 49156
